TPU v7x, 32 devices: a whole 2x2x4 slice. The times are simulated.
32 devices in a mesh: space: 8 (over z, y), dp: 4 (over x, core).
Axes of the slice: x: 2, y: 2, z: 4, core: 2. Of those that a mesh axis runs over, the one named last changes fastest.
Arguments:
- input_states: bfloat16 [4, 8, 200, 1024], P('dp', 'space'), may hold values from -6 to 6
- loss_sensitivity: bfloat16 [4, 8, 200, 1024], P('dp', 'space'), may hold values from -6 to 6
- ocean: int32 [8, 1024], P('space'), may hold values 0 or 1
- neighbours: int32 [8, 8], P('space'), may hold values from -1 to 7, as said below
- fold_flag: int32 [8], P('space'), may hold values from 0 to 1, as said below
- w_first: bfloat16 [9, 200, 200], replicated, may hold values from -0.125 to 0.125
- w_second: bfloat16 [9, 200, 200], replicated, may hold values from -0.125 to 0.125
Outputs:
- prediction: bfloat16 [4, 8, 200, 1024], P('dp', 'space')
- earlier_kernel_slope: float32 [9, 200, 200], replicated
- latter_kernel_slope: float32 [9, 200, 200], replicated
Inputs may be any that keep to these rules, and one draw needn't show every extreme that they name: Tiles sit on a grid of 2 x 16 tile positions, some of them land; the ocean tiles carry numbers 0 to 7 in no particular order of positions; longitude wraps; the top row's northern neighbour is the mirrored tile of the same row (fold_flag 1) and its diagonal northern neighbours are -1. The relation is symmetric: if u is t's neighbour in one direction, t is u's in the opposite one (north for north across the fold). `fold_flag`: 1 exactly for tiles of the top tile row.
All inputs are finite; a program needn't handle non-finite values. No bound on the sum of `ocean` on one device may be relied on, other than what follows from the above.
Results may differ from a plain program's by a relative error of at most 0.005.
Values may be sent and summed in bfloat16 or wider, within the bound.
A program may use at most 64 MiB of HBM per device.

v0:
```python
import jax
import jax.numpy as jnp
from jax import lax
from jax.sharding import PartitionSpec as P

SIDE = 32


SQRT_TWO_PI = 0.7978845608028654
CUBIC = 0.044715


def gelu_pair(a):
    inner = SQRT_TWO_PI * (a + CUBIC * a * a * a)
    tangent = jnp.tanh(inner)
    value = 0.5 * a * (1.0 + tangent)
    slope = 0.5 * (1.0 + tangent) + 0.5 * a * (1.0 - tangent * tangent) * SQRT_TWO_PI * (
        1.0 + 3.0 * CUBIC * a * a
    )
    return (value, slope)


def edge_strips(field):
    patch_extent = field.shape[2]
    return jnp.concatenate(
        [
            field[:, :, 0, :],
            field[:, :, patch_extent - 1, :],
            field[:, :, :, 0],
            field[:, :, :, patch_extent - 1],
        ],
        axis=2,
    )


def strip_parts(piece, neighbours, fold_flag):
    amount = piece.shape[0]
    patch_extent = piece.shape[2] // 4

    def pick(k):
        index = neighbours[:, k]
        valid = ((index >= 0) & (index < amount)).astype(piece.dtype)
        return jnp.take(piece, jnp.clip(index, 0, amount - 1), axis=0) * valid[:, None, None]

    from_north = pick(0)
    north = jnp.where(
        (fold_flag == 1)[:, None, None],
        from_north[:, :, patch_extent : 2 * patch_extent][:, :, ::-1],
        from_north[:, :, 0:patch_extent],
    )
    south = pick(1)[:, :, patch_extent : 2 * patch_extent]
    east = pick(2)[:, :, 2 * patch_extent : 3 * patch_extent]
    west = pick(3)[:, :, 3 * patch_extent : 4 * patch_extent]
    corners = jnp.stack(
        [
            pick(4)[:, :, 0],
            pick(5)[:, :, patch_extent - 1],
            pick(6)[:, :, patch_extent],
            pick(7)[:, :, 2 * patch_extent - 1],
        ],
        axis=-1,
    )
    return (north, south, east, west, corners)


def collect_rims(strips, neighbours, fold_flag):
    found = strip_parts(lax.all_gather(strips, "space", axis=0, tiled=True), neighbours, fold_flag)
    return tuple((b for b in found))


def padded_tiles(field, parts):
    north, south, east, west, corners = parts
    middle = jnp.concatenate([west[..., None], field, east[..., None]], axis=3)
    bottom = jnp.concatenate([corners[:, :, 3:4], south, corners[:, :, 2:3]], axis=2)[:, :, None, :]
    top = jnp.concatenate([corners[:, :, 1:2], north, corners[:, :, 0:1]], axis=2)[:, :, None, :]
    return jnp.concatenate([bottom, middle, top], axis=2)


def window(padded, shift_r, shift_c):
    patch_extent = padded.shape[2] - 2
    part = padded[
        :, :, 1 + shift_r : 1 + shift_r + patch_extent, 1 + shift_c : 1 + shift_c + patch_extent
    ]
    return part.reshape(padded.shape[0], padded.shape[1], patch_extent * patch_extent)


def conv_forward(padded, weights):
    total = None
    for k in range(9):
        term = jnp.einsum(
            "oi,tic->toc",
            weights[k],
            window(padded, k // 3 - 1, k % 3 - 1),
            preferred_element_type=jnp.float32,
        )
        total = term if total is None else total + term
    return total


def conv_adjoint(padded, weights):
    total = None
    for k in range(9):
        term = jnp.einsum(
            "oi,toc->tic",
            weights[k],
            window(padded, 1 - k // 3, 1 - k % 3),
            preferred_element_type=jnp.float32,
        )
        total = term if total is None else total + term
    return total


def weight_grad(grads, padded):
    return jnp.stack(
        [
            jnp.einsum(
                "toc,tic->oi",
                grads,
                window(padded, k // 3 - 1, k % 3 - 1),
                preferred_element_type=jnp.float32,
            )
            for k in range(9)
        ],
        axis=0,
    )


def body(input_states, loss_sensitivity, ocean, neighbours, fold_flag, w_first, w_second):
    tiles = input_states[0]
    patch_total, feature_depth, cells = tiles.shape
    patch_extent = SIDE
    inputs = tiles.reshape(patch_total, feature_depth, patch_extent, patch_extent)
    water_indicator = ocean.astype(jnp.float32)[:, None, :]
    masked_grad = (loss_sensitivity[0].astype(jnp.float32) * water_indicator).astype(jnp.bfloat16)
    grad_tiles = masked_grad.reshape(patch_total, feature_depth, patch_extent, patch_extent)
    field_parts = collect_rims(edge_strips(inputs), neighbours, fold_flag)
    in_padded = padded_tiles(inputs, field_parts)
    pre_first = conv_forward(in_padded, w_first)
    value, slope = gelu_pair(pre_first)
    hidden = (value * water_indicator).astype(jnp.bfloat16)
    hidden_tiles = hidden.reshape(patch_total, feature_depth, patch_extent, patch_extent)
    hidden_parts = collect_rims(edge_strips(hidden_tiles), neighbours, fold_flag)
    hidden_padded = padded_tiles(hidden_tiles, hidden_parts)
    latter_linear_response = conv_forward(hidden_padded, w_second)
    prediction = (latter_linear_response * water_indicator).astype(jnp.bfloat16)[None]
    grad_parts = collect_rims(edge_strips(grad_tiles), neighbours, fold_flag)
    grad_padded = padded_tiles(grad_tiles, grad_parts)
    latter_kernel_slope = weight_grad(masked_grad, hidden_padded)
    back = conv_adjoint(grad_padded, w_second).reshape(
        patch_total, feature_depth, patch_extent, patch_extent
    )
    top_row = grad_padded[:, :, patch_extent + 1, :]
    correction = jnp.zeros((patch_total, feature_depth, patch_extent), jnp.float32)
    for shift_c in (-1, 0, 1):
        segment = top_row[:, :, 1 - shift_c : 1 - shift_c + patch_extent]
        correction = correction + jnp.einsum(
            "oi,toc->tic", w_second[7 - shift_c], segment, preferred_element_type=jnp.float32
        )
        correction = correction - jnp.einsum(
            "oi,toc->tic", w_second[1 + shift_c], segment, preferred_element_type=jnp.float32
        )
    flipped = (fold_flag == 1).astype(jnp.float32)[:, None, None]
    back = back.at[:, :, patch_extent - 1, :].add(correction * flipped)
    pre_grad = (back.reshape(patch_total, feature_depth, cells) * water_indicator * slope).astype(
        jnp.bfloat16
    )
    earlier_kernel_slope = weight_grad(pre_grad, in_padded)
    earlier_kernel_slope, latter_kernel_slope = lax.psum(
        (earlier_kernel_slope, latter_kernel_slope), ("space", "dp")
    )
    return (prediction, earlier_kernel_slope, latter_kernel_slope)


def solution(mesh):
    placed = (
        P("dp", "space", None, None),
        P("dp", "space", None, None),
        P("space", None),
        P("space", None),
        P("space"),
        P(),
        P(),
    )
    return jax.shard_map(
        body,
        mesh=mesh,
        in_specs=placed,
        out_specs=(P("dp", "space", None, None), P(), P()),
        check_vma=False,
    )
```

profile of v0, /device:TPU:1, one launch (start us, length us, event | category | flops | bytes accessed | tf_op | source)
XLA Modules:
  0.0 327.5 jit_solution(8180714459011492790)
XLA Ops:
  8.7 1.6 fusion.168
  25.2 1.2 copy.238
  28.0 26.4 %all_gather.11 = bf16[8,200,128]{2,1,0:T(8,128)(2,1)S(1)} all-gather(bf16[1,200,128]{2,1,0:T(8,128)(2,1)S(1)} %copy.239), channel_id=1, replica_groups=mesh['space'=8,'dp'=4] {'space'}, dimensions={0}, use_global_device_ids=true | all-gather | bytes 460800 | tf_op jit(solution)/shard_map/all_gather | solution.py:67
  56.9 24.9 %all_gather.9 = bf16[8,200,128]{2,1,0:T(8,128)(2,1)S(1)} all-gather(bf16[1,200,128]{2,1,0:T(8,128)(2,1)S(1)} %copy.211), channel_id=1, replica_groups=mesh['space'=8,'dp'=4] {'space'}, dimensions={0}, use_global_device_ids=true | all-gather | bytes 460800 | tf_op jit(solution)/shard_map/all_gather | solution.py:67
  83.5 1.2 pad_maximum_fusion.7
  85.2 1.5 fusion.163
  91.7 1.2 fusion
  93.0 1.5 copy.252
  94.6 1.2 copy.253
  102.4 25.0 %all_gather.10 = bf16[8,200,128]{2,1,0:T(8,128)(2,1)S(1)} all-gather(bf16[1,200,128]{2,1,0:T(8,128)(2,1)S(1)} %copy.225), channel_id=1, replica_groups=mesh['space'=8,'dp'=4] {'space'}, dimensions={0}, use_global_device_ids=true | all-gather | bytes 460800 | tf_op jit(solution)/shard_map/all_gather | solution.py:67
  130.6 1.5 slice.501
  134.7 1.5 slice.499
  137.1 1.5 slice.498
  145.2 1.2 copy-done.18
  147.5 1.2 fusion.14
  148.7 1.2 fusion.13
  149.9 1.2 fusion.12
  151.1 1.2 fusion.11
  153.5 1.2 fusion.9
  154.7 1.2 fusion.8
  155.9 1.2 fusion.7
  162.8 153.6 %all-reduce.3.cloned.1.call-done = (f32[9,200,200]{2,1,0:T(8,128)}, f32[9,200,200]{2,1,0:T(8,128)}) async-done(((f32[9,200,200]{2,1,0:T(8,128)}, f32[9,200,200]{2,1,0:T(8,128)}), (f32[9,200,200]{2,1,0:T(8,128)}, f32[9,200,200]{2,1,0:T(8,128)})) %all-reduce.3.cloned.1.call-update) | async-done | bytes 2880016 | tf_op jit(solution)/shard_map/psum | solution.py:168
  316.4 3.0 copy.333
  319.4 1.2 copy.334
  (229 shorter events, 38.9 us)
Async XLA Ops:
  7.2 19.6 %copy-start.15 = (bf16[1,1,200,1024]{3,2,1,0:T(8,128)(2,1)S(1)}, bf16[1,1,200,1024]{3,2,1,0:T(8,128)(2,1)}, u32[]{:S(2)}) copy-start(bf16[1,1,200,1024]{3,2,1,0:T(8,128)(2,1)} %param.11) | copy-start | bytes 1228804
  7.2 309.3 %all-reduce.3.cloned.1.call-start = ((), (), s32[]{:S(2)}) async-start(), calls=%async_computation | async-start | bytes 7372800 | tf_op jit(solution)/shard_map/psum | solution.py:168
  26.4 28.0 %copy-start.2 = (bf16[1,1,200,1024]{2,3,1,0:T(8,128)(2,1)}, bf16[1,1,200,1024]{2,3,1,0:T(8,128)(2,1)S(1)}, u32[]{:S(2)}) copy-start(bf16[1,1,200,1024]{2,3,1,0:T(8,128)(2,1)S(1)} %copy.238) | copy-start | bytes 1228804
  27.0 29.1 %copy-start = (bf16[9,200,200]{2,1,0:T(8,128)(2,1)S(1)}, bf16[9,200,200]{2,1,0:T(8,128)(2,1)}, u32[]{:S(2)}) copy-start(bf16[9,200,200]{2,1,0:T(8,128)(2,1)} %param.17) | copy-start | bytes 2160004
  95.8 1.2 copy-start.32
  96.2 1.1 copy-start.13
  96.2 1.5 copy-start.11
  96.2 1.5 copy-start.9
  99.0 1.1 copy-start.5
  99.8 1.1 copy-start.25
  99.8 1.3 copy-start.31
  102.0 36.7 %copy-start.28 = (bf16[1,200,1024]{2,1,0:T(8,128)(2,1)}, bf16[1,200,1024]{2,1,0:T(8,128)(2,1)S(1)}, u32[]{:S(2)}) copy-start(bf16[1,200,1024]{2,1,0:T(8,128)(2,1)S(1)} %get-tuple-element.30) | copy-start | bytes 1228804
  140.4 10.6 %copy-start.19 = (bf16[1,200,32,32]{1,3,2,0:T(8,128)(2,1)}, bf16[1,200,32,32]{1,3,2,0:T(8,128)(2,1)S(1)}, u32[]{:S(2)}) copy-start(bf16[1,200,32,32]{1,3,2,0:T(8,128)(2,1)S(1)} %get-tuple-element.62) | copy-start | bytes 1228804
  141.0 1.3 copy-start.12
  141.3 13.3 %copy-start.23 = (bf16[1,200,32,32]{1,3,2,0:T(8,128)(2,1)}, bf16[1,200,32,32]{1,3,2,0:T(8,128)(2,1)S(1)}, u32[]{:S(2)}) copy-start(bf16[1,200,32,32]{1,3,2,0:T(8,128)(2,1)S(1)} %get-tuple-element.39) | copy-start | bytes 1228804
  141.4 14.5 %copy-start.21 = (bf16[1,200,32,32]{1,3,2,0:T(8,128)(2,1)}, bf16[1,200,32,32]{1,3,2,0:T(8,128)(2,1)S(1)}, u32[]{:S(2)}) copy-start(bf16[1,200,32,32]{1,3,2,0:T(8,128)(2,1)S(1)} %get-tuple-element.38) | copy-start | bytes 1228804
  141.4 1.5 copy-start.10
  142.3 1.2 copy-start.17
  143.5 1.1 copy-start.6
  143.8 1.1 copy-start.26
  145.2 1.2 copy-start.18
  149.9 2.4 copy-start.29
  160.3 1.1 copy-start.22
  316.4 3.0 copy-start.27
  (10 other events, 10.5 us)
Sparse Core Ops, SparseCore 0:
  158.4 157.9 all-reduce.2
where the time goes:
time: 331 us; the launch traced here: 328 us
  waiting for transfers between devices  154 us (47%)
  blocking collectives  76.3 us (23%)
  local copies, waits for them, and re-layouts  35.6 us (11%)
  between operations  30.8 us (9%)
  matrix products  25.4 us (8%)
  other arithmetic  5.65 us (2%)
    psum x1, waiting for transfers between devices, body(): lax.psum((earlier_kernel_slope, latter_kernel_slope), ('space', 'dp'))  154 us
    all_gather x3, blocking collectives, collect_rims(): lax.all_gather(strips, 'space', axis=0, tiled=True)  76.3 us
    unnamed x98, local copies, waits for them, and re-layouts  19 us
    dot_general x18, matrix products, weight_grad(): jnp.einsum('toc,tic->oi', grads, window(padded, k // 3 - 1, k % 3 - 1), p...  13.3 us
    dot_general x18, matrix products, conv_forward(): jnp.einsum('oi,tic->toc', weights[k], window(padded, k // 3 - 1, k % 3 -...  7.06 us
  transfers between devices with their start and end apart: 1, of which 1 were waited for; matrix products, arithmetic and copies ran while one was open for 1% of the time, Pallas kernels for 0%

commit v1 on v0

v1 whole, which is shorter than its diff:
```python
import functools

import jax
import jax.numpy as jnp
from jax import lax
from jax.experimental import pallas as pl
from jax.experimental.pallas import tpu as pltpu
from jax.sharding import PartitionSpec as P

SIDE = 32
CELLS = SIDE * SIDE
EXT = CELLS + 2 * SIDE
SQRT_TWO_PI = 0.7978845608028654
CUBIC = 0.044715
F32 = jnp.float32
BF16 = jnp.bfloat16
NN = (((1,), (0,)), ((), ()))
NT = (((1,), (1,)), ((), ()))


def matmul(a, b, dims=NN):
    return lax.dot_general(a, b, dims, preferred_element_type=F32)


def gelu_pair(a):
    inner = SQRT_TWO_PI * (a + CUBIC * a * a * a)
    tangent = jnp.tanh(inner)
    value = 0.5 * a * (1.0 + tangent)
    slope = 0.5 * (1.0 + tangent) + 0.5 * a * (1.0 - tangent * tangent) * SQRT_TWO_PI * (
        1.0 + 3.0 * CUBIC * a * a
    )
    return (value, slope)


def each(count, step):
    if count <= 8:
        for q in range(count):
            step(q)
    else:
        lax.fori_loop(0, count, lambda q, c: (step(q), c)[1], 0)


def kernel(
    n_space, rows,
    x_ref, g_ref, ocean_ref, nb_ref, flag_ref, w1_ref, w2_ref,
    pred_ref, out1_ref, out2_ref,
    gath0, gath1, gath2, pads, hidden_ref, slope_ref, gt_ref, mask_ref, acc, stage, land, res,
    near_send, far_send, strip_recv, red_send, red_recv,
):
    depth = x_ref.shape[0]
    half_n = n_space // 2
    me = lax.axis_index("space")
    dp = lax.axis_index("dp")
    y = me % 2
    z = me // 2
    core = dp % 2
    x = dp // 2
    mate = z * 2 + (1 - y)
    core_mate = x * 2 + (1 - core)
    x_mate = (1 - x) * 2 + core
    mesh_id = pl.DeviceIdType.MESH
    gath = (gath0, gath1, gath2)

    def peer(q):
        return (z + q) % half_n

    def source(q):
        return (z + half_n - q) % half_n

    barrier = pltpu.get_barrier_semaphore()

    def greet(space_to, dp_to):
        pl.semaphore_signal(barrier, inc=1, device_id=(space_to, dp_to), device_id_type=mesh_id)

    each(half_n - 1, lambda q: greet(peer(q + 1) * 2 + y, dp))
    greet(mate, dp)
    greet(me, core_mate)
    greet(me, x_mate)

    def near_copy(f, q):
        return pltpu.make_async_remote_copy(
            src_ref=gath[f].at[me], dst_ref=gath[f].at[me],
            send_sem=near_send.at[f, q], recv_sem=strip_recv.at[f, me],
            device_id=(peer(q) * 2 + y, dp), device_id_type=mesh_id)

    def far_copy(f, q):
        slot = source(q) * 2 + y
        return pltpu.make_async_remote_copy(
            src_ref=gath[f].at[slot], dst_ref=gath[f].at[slot],
            send_sem=far_send.at[f, q], recv_sem=strip_recv.at[f, slot],
            device_id=(mate, dp), device_id_type=mesh_id)

    def arrived(f, slot):
        pltpu.make_async_remote_copy(
            src_ref=gath[f].at[slot], dst_ref=gath[f].at[slot],
            send_sem=near_send.at[f, 0], recv_sem=strip_recv.at[f, slot],
            device_id=(mate, dp), device_id_type=mesh_id).wait_recv()

    def send_own(f):
        each(half_n - 1, lambda q: near_copy(f, q + 1).start())
        far_copy(f, 0).start()

    def forward(f):
        def step(q):
            arrived(f, source(q + 1) * 2 + y)
            far_copy(f, q + 1).start()
        each(half_n - 1, step)

    def collect(f):
        each(half_n, lambda q: arrived(f, source(q) * 2 + (1 - y)))

    def sent(f):
        def step(q):
            near_copy(f, q + 1).wait_send()
        each(half_n - 1, step)
        each(half_n, lambda q: far_copy(f, q).wait_send())

    j = lax.broadcasted_iota(jnp.int32, (4 * SIDE, CELLS), 0)
    c = lax.broadcasted_iota(jnp.int32, (4 * SIDE, CELLS), 1)
    cell = jnp.where(
        j < SIDE, j,
        jnp.where(j < 2 * SIDE, j + (CELLS - 2 * SIDE),
                  jnp.where(j < 3 * SIDE, (j - 2 * SIDE) * SIDE, (j - 3 * SIDE) * SIDE + SIDE - 1)))
    pick = (c == cell).astype(F32).astype(BF16)

    ocean_row = ocean_ref[...].astype(F32)
    gt = (g_ref[...].astype(F32) * ocean_row).astype(BF16)
    gt_ref[...] = gt
    gath0[me] = matmul(pick, x_ref[...], NT).astype(BF16)
    gath1[me] = matmul(pick, gt, NT).astype(BF16)
    pl.semaphore_wait(barrier, half_n + 2)
    send_own(0)
    send_own(1)

    ocean_t = jnp.transpose(jnp.broadcast_to(ocean_row, (128, CELLS)))
    mask_ref[...] = jnp.concatenate([ocean_t, ocean_t], axis=1)[:, :depth]

    fold = flag_ref[0]
    ext_row = lax.broadcasted_iota(jnp.int32, (EXT, 3 * SIDE), 0)
    col = lax.broadcasted_iota(jnp.int32, (EXT, 3 * SIDE), 1)
    line = ext_row // SIDE
    spot = ext_row % SIDE
    last = SIDE + 1
    east_col = jnp.where(line == 0, SIDE, jnp.where(line == last, 2 * SIDE, line - 1))
    west_col = jnp.where(line == 0, 2 * SIDE - 1, jnp.where(line == last, 3 * SIDE - 1, line - 1))
    east_put = ((spot == SIDE - 1) & (col == east_col)).astype(F32).astype(BF16)
    west_put = ((spot == 0) & (col == west_col)).astype(F32).astype(BF16)
    nr = lax.broadcasted_iota(jnp.int32, (SIDE, 2 * SIDE), 0)
    nc = lax.broadcasted_iota(jnp.int32, (SIDE, 2 * SIDE), 1)
    north_put = (nc == jnp.where(fold == 1, 2 * SIDE - 1 - nr, nr)).astype(F32).astype(BF16)
    wide = lax.broadcasted_iota(jnp.int32, (EXT, depth), 0) % SIDE

    def build(f, field):
        def block(k, part, count=1):
            index = nb_ref[0, k]
            valid = (index >= 0).astype(F32)
            got = gath[f][jnp.maximum(index, 0), part * SIDE:(part + count) * SIDE, :]
            return got.astype(F32) * valid

        north = matmul(north_put, block(0, 0, 2).astype(BF16))
        south = block(1, 1)
        ext = jnp.concatenate([south, field, north], axis=0)
        east = jnp.concatenate([block(2, 2), block(6, 1), block(4, 0)], axis=0).astype(BF16)
        west = jnp.concatenate([block(3, 3), block(7, 1), block(5, 0)], axis=0).astype(BF16)
        pads[f, 1] = ext.astype(BF16)
        plus = jnp.where(wide == SIDE - 1, 0.0, pltpu.roll(ext, EXT - 1, 0))
        pads[f, 2] = (plus + matmul(east_put, east)).astype(BF16)
        minus = jnp.where(wide == 0, 0.0, pltpu.roll(ext, 1, 0))
        pads[f, 0] = (minus + matmul(west_put, west)).astype(BF16)

    def window(f, dr, dc):
        start = SIDE * (dr + 1)
        return pads[f, dc + 1, start:start + CELLS, :]

    def conv(f, w_ref):
        total = None
        for k in range(9):
            term = matmul(window(f, k // 3 - 1, k % 3 - 1), w_ref[k], NT)
            total = term if total is None else total + term
        return total

    def weight_grad(s, grads, f):
        for k in range(9):
            acc[s, k * depth:(k + 1) * depth, :] = matmul(grads, window(f, k // 3 - 1, k % 3 - 1))

    ways = (
        ((core, (me, core_mate)), (x, (me, x_mate)), (y, (mate, dp))),
        ((core, (me, core_mate)), (y, (mate, dp)), (x, (me, x_mate))),
    )
    offsets = []
    for s in range(2):
        off = 0
        marks = []
        for t, (bit, _) in enumerate(ways[s]):
            size = rows >> (t + 1)
            marks.append((off + bit * size, off + (1 - bit) * size))
            off = off + bit * size
        offsets.append(marks)
    piece = rows // (8 * half_n)

    def span(start, size):
        return pl.ds(pl.multiple_of(start, 16), size)

    def halve_copy(s, t):
        size = rows >> (t + 1)
        return pltpu.make_async_remote_copy(
            src_ref=stage.at[s, span(offsets[s][t][1], size)],
            dst_ref=land.at[s, pl.ds(rows - 2 * size, size)],
            send_sem=red_send.at[s, t], recv_sem=red_recv.at[s, t],
            device_id=ways[s][t][1], device_id_type=mesh_id)

    def halve_start(s, t):
        size = rows >> (t + 1)
        away = span(offsets[s][t][1], size)
        stage[s, away] = acc[s, away].astype(BF16)
        halve_copy(s, t).start()

    def halve_end(s, t):
        size = rows >> (t + 1)
        halve_copy(s, t).wait_recv()
        keep = span(offsets[s][t][0], size)
        acc[s, keep] = acc[s, keep] + land[s, pl.ds(rows - 2 * size, size)].astype(F32)

    base = rows - rows // 8

    def z_copy(s, q):
        off = offsets[s][2][0]
        return pltpu.make_async_remote_copy(
            src_ref=stage.at[s, span(off + peer(q) * piece, piece)],
            dst_ref=land.at[s, span(base + z * piece, piece)],
            send_sem=red_send.at[s, 6 + q], recv_sem=red_recv.at[s, 6 + q],
            device_id=(peer(q) * 2 + y, dp), device_id_type=mesh_id)

    def z_start(s):
        whole = span(offsets[s][2][0], rows // 8)
        stage[s, whole] = acc[s, whole].astype(BF16)
        each(half_n - 1, lambda q: z_copy(s, q + 1).start())

    def z_end(s):
        mine = span(offsets[s][2][0] + z * piece, piece)

        def step(q):
            z_copy(s, q + 1).wait_recv()
            got = land[s, span(base + source(q + 1) * piece, piece)]
            acc[s, mine] = acc[s, mine] + got.astype(F32)
        each(half_n - 1, step)
        res[s, mine] = acc[s, mine].astype(BF16)

    def zg_copy(s, q):
        mine = span(offsets[s][2][0] + z * piece, piece)
        return pltpu.make_async_remote_copy(
            src_ref=res.at[s, mine], dst_ref=res.at[s, mine],
            send_sem=red_send.at[s, 6 + half_n + q], recv_sem=red_recv.at[s, 6 + half_n + q],
            device_id=(peer(q) * 2 + y, dp), device_id_type=mesh_id)

    def grow_copy(s, t):
        have = span(offsets[s][t][0], rows >> (t + 1))
        return pltpu.make_async_remote_copy(
            src_ref=res.at[s, have], dst_ref=res.at[s, have],
            send_sem=red_send.at[s, 3 + t], recv_sem=red_recv.at[s, 3 + t],
            device_id=ways[s][t][1], device_id_type=mesh_id)

    for s in range(2):
        acc[s, 9 * depth:] = jnp.zeros((rows - 9 * depth, depth), F32)
    forward(0)
    forward(1)
    field_x = jnp.transpose(x_ref[...].astype(F32))
    collect(0)
    build(0, field_x)
    value, slope = gelu_pair(conv(0, w1_ref))
    hidden = (value * mask_ref[...]).astype(BF16)
    hidden_ref[...] = hidden
    slope_ref[...] = slope * mask_ref[...]
    gath2[me] = matmul(pick, hidden).astype(BF16)
    send_own(2)

    field_g = jnp.transpose(gt_ref[...].astype(F32))
    collect(1)
    build(1, field_g)
    forward(2)
    back = None
    edge = None
    for k in (3, 4, 5, 6, 7, 8):
        term = matmul(window(1, 1 - k // 3, 1 - k % 3), w2_ref[k])
        back = term if back is None else back + term
    inner = None
    for k in range(3):
        dc = 1 - k % 3
        term = matmul(pads[1, dc + 1, 2 * SIDE:EXT - SIDE, :], w2_ref[k])
        inner = term if inner is None else inner + term
        across = jnp.where(fold == 1, w2_ref[8 - k].astype(F32), w2_ref[k].astype(F32)).astype(BF16)
        term = matmul(pads[1, dc + 1, EXT - SIDE:EXT, :], across)
        edge = term if edge is None else edge + term
    back = back + jnp.concatenate([inner, edge], axis=0)
    pre_grad = back * slope_ref[...]
    weight_grad(0, jnp.transpose(pre_grad).astype(BF16), 0)
    halve_start(0, 0)

    collect(2)
    build(2, hidden_ref[...].astype(F32))
    weight_grad(1, gt_ref[...], 2)
    halve_start(1, 0)
    halve_end(0, 0)
    halve_start(0, 1)
    forecast = conv(2, w2_ref) * mask_ref[...]
    pred_ref[...] = jnp.transpose(forecast).astype(BF16)
    halve_end(1, 0)
    halve_start(1, 1)
    halve_end(0, 1)
    halve_start(0, 2)
    halve_end(1, 1)
    halve_start(1, 2)
    halve_end(0, 2)
    z_start(0)
    halve_end(1, 2)
    z_start(1)
    for s in range(2):
        z_end(s)
        each(half_n - 1, lambda q: zg_copy(s, q + 1).start())
    for t in (2, 1, 0):
        for s in range(2):
            if t == 2:
                each(half_n - 1, lambda q: zg_copy(s, q + 1).wait_recv())
            else:
                grow_copy(s, t + 1).wait_recv()
            grow_copy(s, t).start()
    out_rows = out1_ref.shape[0]
    for s, out in enumerate((out1_ref, out2_ref)):
        grow_copy(s, 0).wait_recv()
        out[...] = res[s, :out_rows]
    for f in range(3):
        sent(f)
    for s in range(2):
        for t in range(3):
            halve_copy(s, t).wait_send()
            grow_copy(s, t).wait_send()

        def done(q):
            z_copy(s, q + 1).wait_send()
            zg_copy(s, q + 1).wait_send()
        each(half_n - 1, done)


def body(n_space, input_states, loss_sensitivity, ocean, neighbours, fold_flag, w_first, w_second):
    depth = input_states.shape[2]
    half_n = n_space // 2
    unit = 8 * half_n * 16
    used = 9 * depth
    rows = -(-used // unit) * unit
    vmem = pl.BlockSpec(memory_space=pltpu.VMEM)
    smem = pl.BlockSpec(memory_space=pltpu.SMEM)
    prediction, first, second = pl.pallas_call(
        functools.partial(kernel, n_space, rows),
        out_shape=(
            jax.ShapeDtypeStruct((depth, CELLS), BF16),
            jax.ShapeDtypeStruct((used, depth), BF16),
            jax.ShapeDtypeStruct((used, depth), BF16),
        ),
        in_specs=[vmem, vmem, vmem, smem, smem, vmem, vmem],
        out_specs=(vmem, vmem, vmem),
        scratch_shapes=[
            pltpu.VMEM((n_space, 4 * SIDE, depth), BF16),
            pltpu.VMEM((n_space, 4 * SIDE, depth), BF16),
            pltpu.VMEM((n_space, 4 * SIDE, depth), BF16),
            pltpu.VMEM((3, 3, EXT, depth), BF16),
            pltpu.VMEM((CELLS, depth), BF16),
            pltpu.VMEM((CELLS, depth), F32),
            pltpu.VMEM((depth, CELLS), BF16),
            pltpu.VMEM((CELLS, depth), F32),
            pltpu.VMEM((2, rows, depth), F32),
            pltpu.VMEM((2, rows, depth), BF16),
            pltpu.VMEM((2, rows, depth), BF16),
            pltpu.VMEM((2, rows, depth), BF16),
            pltpu.SemaphoreType.DMA((3, half_n)),
            pltpu.SemaphoreType.DMA((3, half_n)),
            pltpu.SemaphoreType.DMA((3, n_space)),
            pltpu.SemaphoreType.DMA((2, 6 + 2 * half_n)),
            pltpu.SemaphoreType.DMA((2, 6 + 2 * half_n)),
        ],
        compiler_params=pltpu.CompilerParams(
            collective_id=0, has_side_effects=True, vmem_limit_bytes=52 * 1024 * 1024),
    )(input_states[0, 0], loss_sensitivity[0, 0], ocean, neighbours, fold_flag, w_first, w_second)
    shape = (9, depth, depth)
    return (
        prediction[None, None],
        first.astype(F32).reshape(shape),
        second.astype(F32).reshape(shape),
    )


def solution(mesh):
    placed = (
        P("dp", "space", None, None),
        P("dp", "space", None, None),
        P("space", None),
        P("space", None),
        P("space"),
        P(),
        P(),
    )
    return jax.shard_map(
        functools.partial(body, mesh.shape["space"]),
        mesh=mesh,
        in_specs=placed,
        out_specs=(P("dp", "space", None, None), P(), P()),
        check_vma=False,
    )
```

time: 331 us -> 87.5 us (0.26)
  waiting for transfers between devices: 154 us -> 0 us
  Pallas kernels: 0 us -> 77.8 us
  blocking collectives: 76.3 us -> 0 us
  local copies, waits for them, and re-layouts: 35.6 us -> 4.09 us
  between operations: 30.8 us -> 1.31 us
  matrix products: 25.4 us -> 0 us
    psum x1 -> x0, waiting for transfers between devices: 154 us -> none  [body(): lax.psum((earlier_kernel_slope, latter_kernel_slope), ('space', 'dp'))]
    pallas_call x0 -> x1, Pallas kernels: none -> 77.8 us  [body(): pl.pallas_call(functools.partial(kernel, n_space, rows), out_shape=(jax.S...]
    all_gather x3 -> x0, blocking collectives: 76.3 us -> none  [collect_rims(): lax.all_gather(strips, 'space', axis=0, tiled=True)]
    dot_general x51 -> x0, matrix products: 25.4 us -> none  [the longest x18 13.3 us: weight_grad(): jnp.einsum('toc,tic->oi', grads, window(padded, k // 3 - 1, k % 3 - 1), p...]
    unnamed x98 -> x11, local copies, waits for them, and re-layouts: 19 us -> 4.09 us
    slice x31 -> x0, local copies, waits for them, and re-layouts: 12.2 us -> none  [the longest x6 3.34 us: window(): padded[:, :, 1 + shift_r:1 + shift_r + patch_extent, 1 + shift_c:1 + shif...]
    reshape x0 -> x2, other arithmetic: none -> 4 us  [the longest x1 2.63 us: body(): first.astype(F32).reshape(shape)]
    concatenate x9 -> x0, other arithmetic: 3.6 us -> none  [the longest x3 2.16 us: padded_tiles(): middle = jnp.concatenate([west[..., None], field, east[..., None]], axis=3)]
  transfers between devices with their start and end apart: 1 -> 0, of which waited for: 1 -> 0; matrix products, arithmetic and copies ran while one was open for 1% -> 0% of each run, Pallas kernels for 0% -> 0%
where the time goes in v1:
time: 87.5 us; the launch traced here: 87.2 us
  Pallas kernels  77.8 us (89%)
  local copies, waits for them, and re-layouts  4.09 us (5%)
  other arithmetic  4 us (5%)
  between operations  1.31 us (1%)
    pallas_call x1, Pallas kernels, body(): pl.pallas_call(functools.partial(kernel, n_space, rows), out_shape=(jax.S...  77.8 us
    unnamed x11, local copies, waits for them, and re-layouts  4.09 us
    reshape x1, other arithmetic, body(): first.astype(F32).reshape(shape)  2.63 us

profile of v1, /device:TPU:1, one launch (start us, length us, event | category | flops | bytes accessed | tf_op | source)
XLA Modules:
  0.0 87.2 jit_solution(8575618894089487234)
XLA Ops:
  1.3 0.0 copy-start
  1.3 1.0 %copy-done = bf16[1,1,200,1024]{3,2,1,0:T(8,128)(2,1)S(1)} copy-done((bf16[1,1,200,1024]{3,2,1,0:T(8,128)(2,1)S(1)}, bf16[1,1,200,1024]{3,2,1,0:T(8,128)(2,1)}, u32[]{:S(2)}) %copy-start) | copy-done | bytes 409624
  2.3 0.0 copy-start.1
  2.3 1.0 %copy-done.1 = bf16[1,1,200,1024]{3,2,1,0:T(8,128)(2,1)S(1)} copy-done((bf16[1,1,200,1024]{3,2,1,0:T(8,128)(2,1)S(1)}, bf16[1,1,200,1024]{3,2,1,0:T(8,128)(2,1)}, u32[]{:S(2)}) %copy-start.1) | copy-done | bytes 409624
  3.3 0.0 copy-start.2
  3.3 0.7 copy-done.2
  4.0 0.0 copy-start.3
  4.0 0.7 copy-done.3
  4.6 77.8 %shard_map.94 = (bf16[200,1024]{1,0:T(8,128)(2,1)S(1)}, bf16[1800,200]{1,0:T(8,128)(2,1)}, bf16[1800,200]{1,0:T(8,128)(2,1)}) custom-call(bf16[200,1024]{1,0:T(8,128)(2,1)S(1)} %bitcast.7, bf16[200,1024]{1,0:T(8,128)(2,1)S(1)} %bitcast.8, s32[1,1024]{1,0:T(1,128)S(1)} %copy-done.2, s32[1,8]{1,0:T(1,128)S(1)} %copy-done.3, s32[1]{0:T(128)S(6)} %copy.11.flag_ref, ...), custom_call_target="tpu_custom_call" | custom-call | tf_op jit(solution)/shard_map/pallas_call | solution.py:352
  82.4 0.0 copy-start.4
  82.4 2.6 %convert.2 = f32[9,200,200]{2,1,0:T(8,128)} convert(bf16[9,200,200]{2,1,0:T(8,128)(2,1)} %bitcast.11) | non-fusion elementwise | flops 360000 | bytes 2160000 | tf_op jit(solution)/shard_map/reshape | solution.py:386
  85.1 0.0 copy-done.4
  85.1 1.4 %convert.3 = f32[9,200,200]{2,1,0:T(8,128)} convert(bf16[9,200,200]{2,1,0:T(8,128)(2,1)S(1)} %bitcast.10) | non-fusion elementwise | flops 360000 | bytes 2160000 | tf_op jit(solution)/shard_map/reshape | solution.py:387
  86.5 0.8 copy.12
Async XLA Ops:
  1.3 1.0 %copy-start = (bf16[1,1,200,1024]{3,2,1,0:T(8,128)(2,1)S(1)}, bf16[1,1,200,1024]{3,2,1,0:T(8,128)(2,1)}, u32[]{:S(2)}) copy-start(bf16[1,1,200,1024]{3,2,1,0:T(8,128)(2,1)} %param.7) | copy-start | bytes 1228804
  2.3 1.0 %copy-start.1 = (bf16[1,1,200,1024]{3,2,1,0:T(8,128)(2,1)S(1)}, bf16[1,1,200,1024]{3,2,1,0:T(8,128)(2,1)}, u32[]{:S(2)}) copy-start(bf16[1,1,200,1024]{3,2,1,0:T(8,128)(2,1)} %param.8) | copy-start | bytes 1228804
  3.3 0.7 copy-start.2
  4.0 0.7 copy-start.3
  82.4 2.6 %copy-start.4 = (bf16[1800,200]{1,0:T(8,128)(2,1)S(1)}, bf16[1800,200]{1,0:T(8,128)(2,1)}, u32[]{:S(2)}) copy-start(bf16[1800,200]{1,0:T(8,128)(2,1)} %get-tuple-element.8) | copy-start | bytes 2160004

commit v2 on v1

--- a/solution.py
+++ b/solution.py
@@ -10,6 +10,7 @@
 SIDE = 32
 CELLS = SIDE * SIDE
 EXT = CELLS + 2 * SIDE
+LANES = 128
 SQRT_TWO_PI = 0.7978845608028654
 CUBIC = 0.044715
 F32 = jnp.float32
@@ -41,7 +42,7 @@
 
 
 def kernel(
-    n_space, rows,
+    n_space, rows, tiles,
     x_ref, g_ref, ocean_ref, nb_ref, flag_ref, w1_ref, w2_ref,
     pred_ref, out1_ref, out2_ref,
     gath0, gath1, gath2, pads, hidden_ref, slope_ref, gt_ref, mask_ref, acc, stage, land, res,
@@ -49,6 +50,7 @@
 ):
     depth = x_ref.shape[0]
     half_n = n_space // 2
+    used = 3 * depth * tiles
     me = lax.axis_index("space")
     dp = lax.axis_index("dp")
     y = me % 2
@@ -180,88 +182,96 @@
         return total
 
     def weight_grad(s, grads, f):
-        for k in range(9):
-            acc[s, k * depth:(k + 1) * depth, :] = matmul(grads, window(f, k // 3 - 1, k % 3 - 1))
-
-    ways = (
-        ((core, (me, core_mate)), (x, (me, x_mate)), (y, (mate, dp))),
-        ((core, (me, core_mate)), (y, (mate, dp)), (x, (me, x_mate))),
-    )
+        for dr in range(3):
+            parts = [matmul(grads, window(f, dr - 1, dc - 1)) for dc in range(3)]
+            spare = jnp.zeros((depth, LANES * tiles - 3 * depth), F32)
+            wide = jnp.concatenate(parts + [spare], axis=1)
+            for t in range(tiles):
+                start = (3 * t + dr) * depth
+                acc[s, start:start + depth, :] = wide[:, LANES * t:LANES * (t + 1)]
+
+    by_core = (core, (me, core_mate))
+    by_x = (x, (me, x_mate))
+    by_y = (y, (mate, dp))
+    ways = ((by_core, by_x, by_y), (by_core, by_y, by_x)) * 2
+    part = rows // 2
     offsets = []
-    for s in range(2):
-        off = 0
+    for u in range(4):
+        off = (u % 2) * part
         marks = []
-        for t, (bit, _) in enumerate(ways[s]):
-            size = rows >> (t + 1)
+        for t, (bit, _) in enumerate(ways[u]):
+            size = part >> (t + 1)
             marks.append((off + bit * size, off + (1 - bit) * size))
             off = off + bit * size
         offsets.append(marks)
-    piece = rows // (8 * half_n)
+    piece = part // (8 * half_n)
 
     def span(start, size):
         return pl.ds(pl.multiple_of(start, 16), size)
 
-    def halve_copy(s, t):
-        size = rows >> (t + 1)
-        return pltpu.make_async_remote_copy(
-            src_ref=stage.at[s, span(offsets[s][t][1], size)],
-            dst_ref=land.at[s, pl.ds(rows - 2 * size, size)],
-            send_sem=red_send.at[s, t], recv_sem=red_recv.at[s, t],
-            device_id=ways[s][t][1], device_id_type=mesh_id)
-
-    def halve_start(s, t):
-        size = rows >> (t + 1)
-        away = span(offsets[s][t][1], size)
-        stage[s, away] = acc[s, away].astype(BF16)
-        halve_copy(s, t).start()
-
-    def halve_end(s, t):
-        size = rows >> (t + 1)
-        halve_copy(s, t).wait_recv()
-        keep = span(offsets[s][t][0], size)
-        acc[s, keep] = acc[s, keep] + land[s, pl.ds(rows - 2 * size, size)].astype(F32)
-
-    base = rows - rows // 8
-
-    def z_copy(s, q):
-        off = offsets[s][2][0]
-        return pltpu.make_async_remote_copy(
-            src_ref=stage.at[s, span(off + peer(q) * piece, piece)],
-            dst_ref=land.at[s, span(base + z * piece, piece)],
-            send_sem=red_send.at[s, 6 + q], recv_sem=red_recv.at[s, 6 + q],
+    def landing(u, t):
+        size = part >> (t + 1)
+        return pl.ds((u % 2) * part + part - 2 * size, size)
+
+    def halve_copy(u, t):
+        return pltpu.make_async_remote_copy(
+            src_ref=stage.at[u // 2, span(offsets[u][t][1], part >> (t + 1))],
+            dst_ref=land.at[u // 2, landing(u, t)],
+            send_sem=red_send.at[u, t], recv_sem=red_recv.at[u, t],
+            device_id=ways[u][t][1], device_id_type=mesh_id)
+
+    def halve_start(u, t):
+        away = span(offsets[u][t][1], part >> (t + 1))
+        stage[u // 2, away] = acc[u // 2, away].astype(BF16)
+        halve_copy(u, t).start()
+
+    def halve_end(u, t):
+        halve_copy(u, t).wait_recv()
+        keep = span(offsets[u][t][0], part >> (t + 1))
+        acc[u // 2, keep] = acc[u // 2, keep] + land[u // 2, landing(u, t)].astype(F32)
+
+    def z_land(u, zp):
+        return span((u % 2) * part + part - part // 8 + zp * piece, piece)
+
+    def z_copy(u, q):
+        off = offsets[u][2][0]
+        return pltpu.make_async_remote_copy(
+            src_ref=stage.at[u // 2, span(off + peer(q) * piece, piece)],
+            dst_ref=land.at[u // 2, z_land(u, z)],
+            send_sem=red_send.at[u, 6 + q], recv_sem=red_recv.at[u, 6 + q],
             device_id=(peer(q) * 2 + y, dp), device_id_type=mesh_id)
 
-    def z_start(s):
-        whole = span(offsets[s][2][0], rows // 8)
-        stage[s, whole] = acc[s, whole].astype(BF16)
-        each(half_n - 1, lambda q: z_copy(s, q + 1).start())
-
-    def z_end(s):
-        mine = span(offsets[s][2][0] + z * piece, piece)
+    def z_start(u):
+        whole = span(offsets[u][2][0], part // 8)
+        stage[u // 2, whole] = acc[u // 2, whole].astype(BF16)
+        each(half_n - 1, lambda q: z_copy(u, q + 1).start())
+
+    def z_end(u):
+        mine = span(offsets[u][2][0] + z * piece, piece)
 
         def step(q):
-            z_copy(s, q + 1).wait_recv()
-            got = land[s, span(base + source(q + 1) * piece, piece)]
-            acc[s, mine] = acc[s, mine] + got.astype(F32)
+            z_copy(u, q + 1).wait_recv()
+            got = land[u // 2, z_land(u, source(q + 1))]
+            acc[u // 2, mine] = acc[u // 2, mine] + got.astype(F32)
         each(half_n - 1, step)
-        res[s, mine] = acc[s, mine].astype(BF16)
-
-    def zg_copy(s, q):
-        mine = span(offsets[s][2][0] + z * piece, piece)
-        return pltpu.make_async_remote_copy(
-            src_ref=res.at[s, mine], dst_ref=res.at[s, mine],
-            send_sem=red_send.at[s, 6 + half_n + q], recv_sem=red_recv.at[s, 6 + half_n + q],
+        res[u // 2, mine] = acc[u // 2, mine].astype(BF16)
+
+    def zg_copy(u, q):
+        mine = span(offsets[u][2][0] + z * piece, piece)
+        return pltpu.make_async_remote_copy(
+            src_ref=res.at[u // 2, mine], dst_ref=res.at[u // 2, mine],
+            send_sem=red_send.at[u, 6 + half_n + q], recv_sem=red_recv.at[u, 6 + half_n + q],
             device_id=(peer(q) * 2 + y, dp), device_id_type=mesh_id)
 
-    def grow_copy(s, t):
-        have = span(offsets[s][t][0], rows >> (t + 1))
-        return pltpu.make_async_remote_copy(
-            src_ref=res.at[s, have], dst_ref=res.at[s, have],
-            send_sem=red_send.at[s, 3 + t], recv_sem=red_recv.at[s, 3 + t],
-            device_id=ways[s][t][1], device_id_type=mesh_id)
+    def grow_copy(u, t):
+        have = span(offsets[u][t][0], part >> (t + 1))
+        return pltpu.make_async_remote_copy(
+            src_ref=res.at[u // 2, have], dst_ref=res.at[u // 2, have],
+            send_sem=red_send.at[u, 3 + t], recv_sem=red_recv.at[u, 3 + t],
+            device_id=ways[u][t][1], device_id_type=mesh_id)
 
     for s in range(2):
-        acc[s, 9 * depth:] = jnp.zeros((rows - 9 * depth, depth), F32)
+        acc[s, used:] = jnp.zeros((rows - used, LANES), F32)
     forward(0)
     forward(1)
     field_x = jnp.transpose(x_ref[...].astype(F32))
@@ -295,66 +305,101 @@
     pre_grad = back * slope_ref[...]
     weight_grad(0, jnp.transpose(pre_grad).astype(BF16), 0)
     halve_start(0, 0)
+    halve_start(1, 0)
 
     collect(2)
     build(2, hidden_ref[...].astype(F32))
+    for u in (0, 1):
+        halve_end(u, 0)
+        halve_start(u, 1)
     weight_grad(1, gt_ref[...], 2)
-    halve_start(1, 0)
-    halve_end(0, 0)
-    halve_start(0, 1)
+    halve_start(2, 0)
+    halve_start(3, 0)
+    for u in (0, 1):
+        halve_end(u, 1)
+        halve_start(u, 2)
     forecast = conv(2, w2_ref) * mask_ref[...]
+    for u in (2, 3):
+        halve_end(u, 0)
+        halve_start(u, 1)
+    for u in (0, 1):
+        halve_end(u, 2)
+        z_start(u)
     pred_ref[...] = jnp.transpose(forecast).astype(BF16)
-    halve_end(1, 0)
-    halve_start(1, 1)
-    halve_end(0, 1)
-    halve_start(0, 2)
-    halve_end(1, 1)
-    halve_start(1, 2)
-    halve_end(0, 2)
-    z_start(0)
-    halve_end(1, 2)
-    z_start(1)
-    for s in range(2):
-        z_end(s)
-        each(half_n - 1, lambda q: zg_copy(s, q + 1).start())
-    for t in (2, 1, 0):
-        for s in range(2):
-            if t == 2:
-                each(half_n - 1, lambda q: zg_copy(s, q + 1).wait_recv())
-            else:
-                grow_copy(s, t + 1).wait_recv()
-            grow_copy(s, t).start()
-    out_rows = out1_ref.shape[0]
-    for s, out in enumerate((out1_ref, out2_ref)):
-        grow_copy(s, 0).wait_recv()
-        out[...] = res[s, :out_rows]
+    for u in (2, 3):
+        halve_end(u, 1)
+        halve_start(u, 2)
+
+    def finish(u):
+        z_end(u)
+        each(half_n - 1, lambda q: zg_copy(u, q + 1).start())
+
+    def grow(u, t):
+        if t == 2:
+            each(half_n - 1, lambda q: zg_copy(u, q + 1).wait_recv())
+        else:
+            grow_copy(u, t + 1).wait_recv()
+        grow_copy(u, t).start()
+
+    def unpack(s, out):
+        grow_copy(2 * s, 0).wait_recv()
+        grow_copy(2 * s + 1, 0).wait_recv()
+        total = res[s].astype(F32)
+        for dr in range(3):
+            starts = [(3 * t + dr) * depth for t in range(tiles)]
+            wide = jnp.concatenate([total[r:r + depth] for r in starts], axis=1)
+            for dc in range(3):
+                out[3 * dr + dc] = wide[:, dc * depth:(dc + 1) * depth].astype(BF16)
+
+    finish(0)
+    finish(1)
+    for u in (2, 3):
+        halve_end(u, 2)
+        z_start(u)
+    grow(0, 2)
+    grow(1, 2)
+    finish(2)
+    finish(3)
+    grow(0, 1)
+    grow(1, 1)
+    grow(2, 2)
+    grow(3, 2)
+    grow(0, 0)
+    grow(1, 0)
+    grow(2, 1)
+    grow(3, 1)
+    unpack(0, out1_ref)
+    grow(2, 0)
+    grow(3, 0)
+    unpack(1, out2_ref)
     for f in range(3):
         sent(f)
-    for s in range(2):
+    for u in range(4):
         for t in range(3):
-            halve_copy(s, t).wait_send()
-            grow_copy(s, t).wait_send()
+            halve_copy(u, t).wait_send()
+            grow_copy(u, t).wait_send()
 
         def done(q):
-            z_copy(s, q + 1).wait_send()
-            zg_copy(s, q + 1).wait_send()
+            z_copy(u, q + 1).wait_send()
+            zg_copy(u, q + 1).wait_send()
         each(half_n - 1, done)
 
 
 def body(n_space, input_states, loss_sensitivity, ocean, neighbours, fold_flag, w_first, w_second):
     depth = input_states.shape[2]
     half_n = n_space // 2
-    unit = 8 * half_n * 16
-    used = 9 * depth
+    unit = 16 * half_n * 16
+    tiles = -(-3 * depth // LANES)
+    used = 3 * depth * tiles
     rows = -(-used // unit) * unit
     vmem = pl.BlockSpec(memory_space=pltpu.VMEM)
     smem = pl.BlockSpec(memory_space=pltpu.SMEM)
     prediction, first, second = pl.pallas_call(
-        functools.partial(kernel, n_space, rows),
+        functools.partial(kernel, n_space, rows, tiles),
         out_shape=(
             jax.ShapeDtypeStruct((depth, CELLS), BF16),
-            jax.ShapeDtypeStruct((used, depth), BF16),
-            jax.ShapeDtypeStruct((used, depth), BF16),
+            jax.ShapeDtypeStruct((9, depth, depth), BF16),
+            jax.ShapeDtypeStruct((9, depth, depth), BF16),
         ),
         in_specs=[vmem, vmem, vmem, smem, smem, vmem, vmem],
         out_specs=(vmem, vmem, vmem),
@@ -367,25 +412,20 @@
             pltpu.VMEM((CELLS, depth), F32),
             pltpu.VMEM((depth, CELLS), BF16),
             pltpu.VMEM((CELLS, depth), F32),
-            pltpu.VMEM((2, rows, depth), F32),
-            pltpu.VMEM((2, rows, depth), BF16),
-            pltpu.VMEM((2, rows, depth), BF16),
-            pltpu.VMEM((2, rows, depth), BF16),
+            pltpu.VMEM((2, rows, LANES), F32),
+            pltpu.VMEM((2, rows, LANES), BF16),
+            pltpu.VMEM((2, rows, LANES), BF16),
+            pltpu.VMEM((2, rows, LANES), BF16),
             pltpu.SemaphoreType.DMA((3, half_n)),
             pltpu.SemaphoreType.DMA((3, half_n)),
             pltpu.SemaphoreType.DMA((3, n_space)),
-            pltpu.SemaphoreType.DMA((2, 6 + 2 * half_n)),
-            pltpu.SemaphoreType.DMA((2, 6 + 2 * half_n)),
+            pltpu.SemaphoreType.DMA((4, 6 + 2 * half_n)),
+            pltpu.SemaphoreType.DMA((4, 6 + 2 * half_n)),
         ],
         compiler_params=pltpu.CompilerParams(
-            collective_id=0, has_side_effects=True, vmem_limit_bytes=52 * 1024 * 1024),
+            collective_id=0, has_side_effects=True, vmem_limit_bytes=(32 + n_space // 4) * 1024 * 1024),
     )(input_states[0, 0], loss_sensitivity[0, 0], ocean, neighbours, fold_flag, w_first, w_second)
-    shape = (9, depth, depth)
-    return (
-        prediction[None, None],
-        first.astype(F32).reshape(shape),
-        second.astype(F32).reshape(shape),
-    )
+    return (prediction[None, None], first.astype(F32), second.astype(F32))
 
 
 def solution(mesh):

time: 87.5 us -> 78.2 us (0.89)
  Pallas kernels: 77.8 us -> 67.4 us
  local copies, waits for them, and re-layouts: 4.09 us -> 6.45 us
  other arithmetic: 4 us -> 2.74 us
    pallas_call x1, Pallas kernels: 77.8 us -> 67.4 us  [body(): pl.pallas_call(functools.partial(kernel, n_space, rows, tiles), out_shape...]
    reshape x2 -> x0, other arithmetic: 4 us -> none  [the longest x1 2.63 us: body(): first.astype(F32).reshape(shape)]
    convert_element_type x0 -> x2, other arithmetic: none -> 2.74 us  [body(): return (prediction[None, None], first.astype(F32), second.astype(F32))]
    unnamed x11 -> x13, local copies, waits for them, and re-layouts: 4.09 us -> 6.45 us
where the time goes in v2:
time: 78.2 us; the launch traced here: 77.9 us
  Pallas kernels  67.4 us (86%)
  local copies, waits for them, and re-layouts  6.45 us (8%)
  other arithmetic  2.74 us (4%)
  between operations  1.3 us (2%)
    pallas_call x1, Pallas kernels, body(): pl.pallas_call(functools.partial(kernel, n_space, rows, tiles), out_shape...  67.4 us
    unnamed x13, local copies, waits for them, and re-layouts  6.45 us
    convert_element_type x2, other arithmetic, body(): return (prediction[None, None], first.astype(F32), second.astype(F32))  2.74 us

profile of v2, /device:TPU:1, one launch (start us, length us, event | category | flops | bytes accessed | tf_op | source)
XLA Modules:
  0.0 77.9 jit_solution(10471554109577269512)
XLA Ops:
  1.3 0.0 copy-start
  1.3 1.2 %copy-done = bf16[9,200,200]{2,1,0:T(8,128)(2,1)S(1)} copy-done((bf16[9,200,200]{2,1,0:T(8,128)(2,1)S(1)}, bf16[9,200,200]{2,1,0:T(8,128)(2,1)}, u32[]{:S(2)}) %copy-start) | copy-done | bytes 720024
  2.5 0.0 copy-start.1
  2.5 1.2 %copy-done.1 = bf16[9,200,200]{2,1,0:T(8,128)(2,1)S(1)} copy-done((bf16[9,200,200]{2,1,0:T(8,128)(2,1)S(1)}, bf16[9,200,200]{2,1,0:T(8,128)(2,1)}, u32[]{:S(2)}) %copy-start.1) | copy-done | bytes 720024
  3.6 0.0 copy-start.2
  3.6 1.0 %copy-done.2 = bf16[1,1,200,1024]{3,2,1,0:T(8,128)(2,1)S(1)} copy-done((bf16[1,1,200,1024]{3,2,1,0:T(8,128)(2,1)S(1)}, bf16[1,1,200,1024]{3,2,1,0:T(8,128)(2,1)}, u32[]{:S(2)}) %copy-start.2) | copy-done | bytes 409624
  4.6 0.0 copy-start.3
  4.6 1.0 %copy-done.3 = bf16[1,1,200,1024]{3,2,1,0:T(8,128)(2,1)S(1)} copy-done((bf16[1,1,200,1024]{3,2,1,0:T(8,128)(2,1)S(1)}, bf16[1,1,200,1024]{3,2,1,0:T(8,128)(2,1)}, u32[]{:S(2)}) %copy-start.3) | copy-done | bytes 409624
  5.6 0.0 copy-start.4
  5.6 0.7 copy-done.4
  6.3 0.0 copy-start.5
  6.3 0.7 copy-done.5
  7.0 67.4 %shard_map.94 = (bf16[200,1024]{1,0:T(8,128)(2,1)S(1)}, bf16[9,200,200]{2,1,0:T(8,128)(2,1)S(1)}, bf16[9,200,200]{2,1,0:T(8,128)(2,1)S(1)}) custom-call(bf16[200,1024]{1,0:T(8,128)(2,1)S(1)} %bitcast.3, bf16[200,1024]{1,0:T(8,128)(2,1)S(1)} %bitcast.4, s32[1,1024]{1,0:T(1,128)S(1)} %copy-done.4, s32[1,8]{1,0:T(1,128)S(1)} %copy-done.5, s32[1]{0:T(128)S(6)} %copy.11.flag_ref, ...), custom_call_target="tpu_custom_call" | custom-call | tf_op jit(solution)/shard_map/pallas_call | solution.py:397
  74.4 1.4 %convert_element_type.6 = f32[9,200,200]{2,1,0:T(8,128)} convert(bf16[9,200,200]{2,1,0:T(8,128)(2,1)S(1)} %get-tuple-element.7) | non-fusion elementwise | flops 360000 | bytes 2160000 | tf_op jit(solution)/shard_map/convert_element_type | solution.py:428
  75.8 1.4 %convert_element_type.7 = f32[9,200,200]{2,1,0:T(8,128)} convert(bf16[9,200,200]{2,1,0:T(8,128)(2,1)S(1)} %get-tuple-element.8) | non-fusion elementwise | flops 360000 | bytes 2160000 | tf_op jit(solution)/shard_map/convert_element_type | solution.py:428
  77.1 0.8 copy.12
Async XLA Ops:
  1.3 1.2 %copy-start = (bf16[9,200,200]{2,1,0:T(8,128)(2,1)S(1)}, bf16[9,200,200]{2,1,0:T(8,128)(2,1)}, u32[]{:S(2)}) copy-start(bf16[9,200,200]{2,1,0:T(8,128)(2,1)} %w1_ref.1) | copy-start | bytes 2160004
  2.5 1.2 %copy-start.1 = (bf16[9,200,200]{2,1,0:T(8,128)(2,1)S(1)}, bf16[9,200,200]{2,1,0:T(8,128)(2,1)}, u32[]{:S(2)}) copy-start(bf16[9,200,200]{2,1,0:T(8,128)(2,1)} %w2_ref.1) | copy-start | bytes 2160004
  3.6 1.0 %copy-start.2 = (bf16[1,1,200,1024]{3,2,1,0:T(8,128)(2,1)S(1)}, bf16[1,1,200,1024]{3,2,1,0:T(8,128)(2,1)}, u32[]{:S(2)}) copy-start(bf16[1,1,200,1024]{3,2,1,0:T(8,128)(2,1)} %param.7) | copy-start | bytes 1228804
  4.6 1.0 %copy-start.3 = (bf16[1,1,200,1024]{3,2,1,0:T(8,128)(2,1)S(1)}, bf16[1,1,200,1024]{3,2,1,0:T(8,128)(2,1)}, u32[]{:S(2)}) copy-start(bf16[1,1,200,1024]{3,2,1,0:T(8,128)(2,1)} %param.8) | copy-start | bytes 1228804
  5.6 0.7 copy-start.4
  6.3 0.7 copy-start.5

commit v3 on v2

--- a/solution.py
+++ b/solution.py
@@ -43,10 +43,10 @@
 
 def kernel(
     n_space, rows, tiles,
-    x_ref, g_ref, ocean_ref, nb_ref, flag_ref, w1_ref, w2_ref,
+    x_ref, g_ref, ocean_ref, nb_ref, flag_ref, w1_far, w2_far,
     pred_ref, out1_ref, out2_ref,
-    gath0, gath1, gath2, pads, hidden_ref, slope_ref, gt_ref, mask_ref, acc, stage, land, res,
-    near_send, far_send, strip_recv, red_send, red_recv,
+    gath0, gath1, gath2, pads, hidden_ref, slope_ref, gt_ref, mask_ref, acc, stage, land, res, w1_ref, w2_ref,
+    near_send, far_send, strip_recv, red_send, red_recv, load_sem,
 ):
     depth = x_ref.shape[0]
     half_n = n_space // 2
@@ -69,6 +69,10 @@
     def source(q):
         return (z + half_n - q) % half_n
 
+    load1 = pltpu.make_async_copy(w1_far, w1_ref, load_sem.at[0])
+    load2 = pltpu.make_async_copy(w2_far, w2_ref, load_sem.at[1])
+    load1.start()
+    load2.start()
     barrier = pltpu.get_barrier_semaphore()
 
     def greet(space_to, dp_to):
@@ -132,7 +136,6 @@
     gath1[me] = matmul(pick, gt, NT).astype(BF16)
     pl.semaphore_wait(barrier, half_n + 2)
     send_own(0)
-    send_own(1)
 
     ocean_t = jnp.transpose(jnp.broadcast_to(ocean_row, (128, CELLS)))
     mask_ref[...] = jnp.concatenate([ocean_t, ocean_t], axis=1)[:, :depth]
@@ -273,10 +276,12 @@
     for s in range(2):
         acc[s, used:] = jnp.zeros((rows - used, LANES), F32)
     forward(0)
-    forward(1)
+    send_own(1)
     field_x = jnp.transpose(x_ref[...].astype(F32))
     collect(0)
     build(0, field_x)
+    forward(1)
+    load1.wait()
     value, slope = gelu_pair(conv(0, w1_ref))
     hidden = (value * mask_ref[...]).astype(BF16)
     hidden_ref[...] = hidden
@@ -287,6 +292,7 @@
     field_g = jnp.transpose(gt_ref[...].astype(F32))
     collect(1)
     build(1, field_g)
+    load2.wait()
     forward(2)
     back = None
     edge = None
@@ -394,6 +400,7 @@
     rows = -(-used // unit) * unit
     vmem = pl.BlockSpec(memory_space=pltpu.VMEM)
     smem = pl.BlockSpec(memory_space=pltpu.SMEM)
+    hbm = pl.BlockSpec(memory_space=pltpu.HBM)
     prediction, first, second = pl.pallas_call(
         functools.partial(kernel, n_space, rows, tiles),
         out_shape=(
@@ -401,7 +408,7 @@
             jax.ShapeDtypeStruct((9, depth, depth), BF16),
             jax.ShapeDtypeStruct((9, depth, depth), BF16),
         ),
-        in_specs=[vmem, vmem, vmem, smem, smem, vmem, vmem],
+        in_specs=[vmem, vmem, vmem, smem, smem, hbm, hbm],
         out_specs=(vmem, vmem, vmem),
         scratch_shapes=[
             pltpu.VMEM((n_space, 4 * SIDE, depth), BF16),
@@ -416,11 +423,14 @@
             pltpu.VMEM((2, rows, LANES), BF16),
             pltpu.VMEM((2, rows, LANES), BF16),
             pltpu.VMEM((2, rows, LANES), BF16),
+            pltpu.VMEM((9, depth, depth), BF16),
+            pltpu.VMEM((9, depth, depth), BF16),
             pltpu.SemaphoreType.DMA((3, half_n)),
             pltpu.SemaphoreType.DMA((3, half_n)),
             pltpu.SemaphoreType.DMA((3, n_space)),
             pltpu.SemaphoreType.DMA((4, 6 + 2 * half_n)),
             pltpu.SemaphoreType.DMA((4, 6 + 2 * half_n)),
+            pltpu.SemaphoreType.DMA((2,)),
         ],
         compiler_params=pltpu.CompilerParams(
             collective_id=0, has_side_effects=True, vmem_limit_bytes=(32 + n_space // 4) * 1024 * 1024),

time: 78.2 us -> 76.2 us (0.974)
  Pallas kernels: 67.4 us -> 65.4 us
    pallas_call x1, Pallas kernels: 67.4 us -> 65.4 us  [body(): pl.pallas_call(functools.partial(kernel, n_space, rows, tiles), out_shape...]
where the time goes in v3:
time: 76.2 us; the launch traced here: 75.9 us
  Pallas kernels  65.4 us (86%)
  local copies, waits for them, and re-layouts  6.45 us (8%)
  other arithmetic  2.74 us (4%)
  between operations  1.3 us (2%)
    pallas_call x1, Pallas kernels, body(): pl.pallas_call(functools.partial(kernel, n_space, rows, tiles), out_shape...  65.4 us
    unnamed x13, local copies, waits for them, and re-layouts  6.45 us
    convert_element_type x2, other arithmetic, body(): return (prediction[None, None], first.astype(F32), second.astype(F32))  2.74 us

profile of v3, /device:TPU:1, one launch (start us, length us, event | category | flops | bytes accessed | tf_op | source)
XLA Modules:
  0.0 75.9 jit_solution(8172131874054437295)
XLA Ops:
  1.3 0.0 copy-start
  1.3 1.2 %copy-done = bf16[9,200,200]{2,1,0:T(8,128)(2,1)S(1)} copy-done((bf16[9,200,200]{2,1,0:T(8,128)(2,1)S(1)}, bf16[9,200,200]{2,1,0:T(8,128)(2,1)}, u32[]{:S(2)}) %copy-start) | copy-done | bytes 720024
  2.5 0.0 copy-start.1
  2.5 1.2 %copy-done.1 = bf16[9,200,200]{2,1,0:T(8,128)(2,1)S(1)} copy-done((bf16[9,200,200]{2,1,0:T(8,128)(2,1)S(1)}, bf16[9,200,200]{2,1,0:T(8,128)(2,1)}, u32[]{:S(2)}) %copy-start.1) | copy-done | bytes 720024
  3.6 0.0 copy-start.2
  3.6 1.0 %copy-done.2 = bf16[1,1,200,1024]{3,2,1,0:T(8,128)(2,1)S(1)} copy-done((bf16[1,1,200,1024]{3,2,1,0:T(8,128)(2,1)S(1)}, bf16[1,1,200,1024]{3,2,1,0:T(8,128)(2,1)}, u32[]{:S(2)}) %copy-start.2) | copy-done | bytes 409624
  4.6 0.0 copy-start.3
  4.6 1.0 %copy-done.3 = bf16[1,1,200,1024]{3,2,1,0:T(8,128)(2,1)S(1)} copy-done((bf16[1,1,200,1024]{3,2,1,0:T(8,128)(2,1)S(1)}, bf16[1,1,200,1024]{3,2,1,0:T(8,128)(2,1)}, u32[]{:S(2)}) %copy-start.3) | copy-done | bytes 409624
  5.6 0.0 copy-start.4
  5.6 0.7 copy-done.4
  6.3 0.0 copy-start.5
  6.3 0.7 copy-done.5
  7.0 65.4 %shard_map.94 = (bf16[200,1024]{1,0:T(8,128)(2,1)S(1)}, bf16[9,200,200]{2,1,0:T(8,128)(2,1)S(1)}, bf16[9,200,200]{2,1,0:T(8,128)(2,1)S(1)}) custom-call(bf16[200,1024]{1,0:T(8,128)(2,1)S(1)} %bitcast.3, bf16[200,1024]{1,0:T(8,128)(2,1)S(1)} %bitcast.4, s32[1,1024]{1,0:T(1,128)S(1)} %copy-done.4, s32[1,8]{1,0:T(1,128)S(1)} %copy-done.5, s32[1]{0:T(128)S(6)} %copy.11.flag_ref, ...), custom_call_target="tpu_custom_call" | custom-call | tf_op jit(solution)/shard_map/pallas_call | solution.py:404
  72.4 1.4 %convert_element_type.6 = f32[9,200,200]{2,1,0:T(8,128)} convert(bf16[9,200,200]{2,1,0:T(8,128)(2,1)S(1)} %get-tuple-element.7) | non-fusion elementwise | flops 360000 | bytes 2160000 | tf_op jit(solution)/shard_map/convert_element_type | solution.py:438
  73.8 1.4 %convert_element_type.7 = f32[9,200,200]{2,1,0:T(8,128)} convert(bf16[9,200,200]{2,1,0:T(8,128)(2,1)S(1)} %get-tuple-element.8) | non-fusion elementwise | flops 360000 | bytes 2160000 | tf_op jit(solution)/shard_map/convert_element_type | solution.py:438
  75.2 0.8 copy.12
Async XLA Ops:
  1.3 1.2 %copy-start = (bf16[9,200,200]{2,1,0:T(8,128)(2,1)S(1)}, bf16[9,200,200]{2,1,0:T(8,128)(2,1)}, u32[]{:S(2)}) copy-start(bf16[9,200,200]{2,1,0:T(8,128)(2,1)} %w1_far.1) | copy-start | bytes 2160004
  2.5 1.2 %copy-start.1 = (bf16[9,200,200]{2,1,0:T(8,128)(2,1)S(1)}, bf16[9,200,200]{2,1,0:T(8,128)(2,1)}, u32[]{:S(2)}) copy-start(bf16[9,200,200]{2,1,0:T(8,128)(2,1)} %w2_far.1) | copy-start | bytes 2160004
  3.6 1.0 %copy-start.2 = (bf16[1,1,200,1024]{3,2,1,0:T(8,128)(2,1)S(1)}, bf16[1,1,200,1024]{3,2,1,0:T(8,128)(2,1)}, u32[]{:S(2)}) copy-start(bf16[1,1,200,1024]{3,2,1,0:T(8,128)(2,1)} %param.7) | copy-start | bytes 1228804
  4.6 1.0 %copy-start.3 = (bf16[1,1,200,1024]{3,2,1,0:T(8,128)(2,1)S(1)}, bf16[1,1,200,1024]{3,2,1,0:T(8,128)(2,1)}, u32[]{:S(2)}) copy-start(bf16[1,1,200,1024]{3,2,1,0:T(8,128)(2,1)} %param.8) | copy-start | bytes 1228804
  5.6 0.7 copy-start.4
  6.3 0.7 copy-start.5
